TPU v7x, 512 devices: a whole 4x8x8 slice. The times are simulated.
512 devices in a mesh: row: 32 (over y, z_lo), col: 16 (over z_hi, x, core).
Axes of the slice: x: 4, y: 8, z: 8 (z_hi: 2, z_lo: 4; z = z_hi * 4 + z_lo), core: 2. Of those that a mesh axis runs over, the one named last changes fastest.
Arguments:
- signal: bfloat16 [8, 1024, 2048], P(None, 'row', 'col'), may hold values from -6 to 6
- filter_real: bfloat16 [8, 1024, 2048], P(None, 'row', 'col'), may hold values from -6 to 6
- filter_imag: bfloat16 [8, 1024, 2048], P(None, 'row', 'col'), may hold values from -6 to 6
- skip: float32 [8], replicated, may hold values from 0.5 to 1.5
Outputs:
- output: bfloat16 [8, 1024, 2048], P(None, 'row', 'col')
All inputs are finite; a program needn't handle non-finite values.
Results may differ from a plain program's by a relative error of at most 0.0064.
Values may be sent and summed in bfloat16 or wider, within the bound.
A program may use at most 64 MiB of HBM per device.

v0:
```python
import functools

import jax
import jax.numpy as jnp
import numpy as np
from jax import lax
from jax.experimental import pallas as pl
from jax.experimental.pallas import tpu as pltpu
from jax.sharding import PartitionSpec as P

MESH = pl.DeviceIdType.MESH
F32, BF16 = jnp.float32, jnp.bfloat16
N1, N2 = 1024, 2048
SEQ = N1 * N2


def unit(product, modulus):
    angle = 2.0 * np.pi / modulus * (product % modulus)
    return np.cos(angle), np.sin(angle)


def tables():
    g = lambda *dims: np.meshgrid(*[np.arange(n) for n in dims], indexing="ij")
    bl, ka, dl, dh, kb, r, i = g(4, 4, 8, 2, 4, 32, 8)
    k1 = 16 * (8 * bl + dl + 32 * dh) + 4 * ka + kb
    c, s = unit(k1 * (32 * r + i), N1)
    first = np.stack([c, -s], axis=1).reshape(4, 512, 256)
    ka, dl, dh, kb, k, j = g(4, 8, 2, 4, 4, 32)
    c, s = unit((16 * (dl + 32 * dh) + 4 * ka + kb) * 8 * k, N1)
    turn = np.stack([c, -s]).reshape(2, 4, 64, 128)
    c, s = unit(np.outer(np.arange(64), np.arange(64)), 64)
    wide = np.einsum("pqks,bc->pbksqc", np.array([[c, s], [-s, c]]), np.eye(4)).reshape(512, 512)
    ks, ka, j = g(64, 4, 32)
    c, s = unit(j * ks, N2)
    bend = np.stack([c, -s]).reshape(2, 64, 128)
    j, kj0, q = g(32, 2, 16)
    c, s = unit(j * (2 * q + kj0), 32)
    short = np.einsum("pqjhx,ab->pajqhbx", np.array([[c, -s], [s, c]]), np.eye(4)).reshape(256, 256)
    half = lambda a: np.asarray(a, np.float32).astype(BF16)
    full = lambda a: np.asarray(a, np.float32)
    return (
        half(first),
        half(first.reshape(2048, 256).T),
        full(turn),
        half(wide),
        half(wide.T),
        full(bend),
        half(short),
        half(short.T),
    )


def far_first(step, size):
    half = (step + 1) >> 1
    return (size // 2 + jnp.where((step & 1) == 1, -half, half)) & (size - 1)


def kernel(
    signal, filt_re, filt_im, skip,
    c_first, c_back, c_turn, c_wide, c_wideb, c_bend, c_short, c_shortb,
    out,
    x_in, out1, in1, out2, in2, out3, in3, out4, in4, filt_in, filt_f, filt_h, twist, mixed,
    first, back, turn, wide, wideb, bend, short, shortb,
    load_sem, send_sem, recv_sem,
):
    row, col = lax.axis_index("row"), lax.axis_index("col")
    y, zl = row >> 2, row & 3
    z, xs, core = ((col >> 3) << 2) | zl, (col >> 1) & 3, col & 1
    col_id = 4 * col + zl
    freq_id = 8 * (col >> 1) + 2 * zl + core

    loads = [
        pltpu.make_async_copy(a, b, load_sem.at[n])
        for n, (a, b) in enumerate((
            (signal, x_in), (c_first, first), (c_turn, turn), (c_wide, wide), (c_bend, bend),
            (c_short, short), (c_shortb, shortb), (c_wideb, wideb), (c_back, back),
        ))
    ]
    for load in loads:
        load.start()

    def row_peer(u):
        r2 = (((y + far_first(u >> 2, 8)) & 7) << 2) | ((zl + 3 - (u & 3)) & 3)
        return r2, (r2, col)

    def plane_peer(u):
        z2 = (z + far_first(u >> 3, 8)) & 7
        x2 = (xs + far_first((u >> 1) & 3, 4)) & 3
        zl2, col2 = z2 & 3, ((z2 >> 2) << 3) | (x2 << 1) | (core ^ 1 ^ (u & 1))
        return 4 * col2 + zl2, 8 * (col2 >> 1) + 2 * zl2 + (col2 & 1), (4 * y + zl2, col2)

    own = (col >> 1) == y
    barrier = pltpu.get_barrier_semaphore()

    @pl.loop(0, 31)
    def _(u):
        pl.semaphore_signal(barrier, inc=1, device_id=row_peer(u)[1], device_id_type=MESH)

    @pl.loop(0, 63)
    def _(u):
        pl.semaphore_signal(barrier, inc=1, device_id=plane_peer(u)[2], device_id_type=MESH)

    @pl.loop(0, 16)
    def _(u):
        @pl.when(jnp.logical_not(own & (u == col)))
        def _():
            pl.semaphore_signal(
                barrier, inc=1, device_id=(4 * (col >> 1) + zl, u), device_id_type=MESH
            )

    lane = lax.broadcasted_iota(jnp.int32, (8, 128), 1)
    low64, low32 = lane < 64, (lane & 32) == 0
    low4 = lax.broadcasted_iota(jnp.int32, (8, 128), 0) < 4

    def regroup(a):
        u = [[None, None], [None, None]]
        for e in range(2):
            u[0][e] = jnp.where(low64, a[e], pltpu.roll(a[2 + e], 64, 2))
            u[1][e] = jnp.where(low64, pltpu.roll(a[e], 64, 2), a[2 + e])
        v = []
        for b in range(2):
            v.append(jnp.where(low32, u[b][0], pltpu.roll(u[b][1], 32, 2)))
            v.append(jnp.where(low32, pltpu.roll(u[b][0], 96, 2), u[b][1]))
        return v

    loads[0].wait()
    pieces = x_in[...].astype(F32)
    for b, piece in enumerate(regroup([pieces[:, 8 * k : 8 * k + 8, :] for k in range(4)])):
        out1[:, b] = piece.astype(BF16)
    in1[row] = out1[y, zl]

    pl.semaphore_wait(barrier, 31 + 63 + 16 - own.astype(jnp.int32))

    def send1(u):
        r2, device = row_peer(u)
        return pltpu.make_async_remote_copy(
            src_ref=out1.at[r2 >> 2, r2 & 3], dst_ref=in1.at[row],
            send_sem=send_sem.at[0], recv_sem=recv_sem.at[0], device_id=device, device_id_type=MESH,
        )

    @pl.loop(0, 31)
    def _(u):
        send1(u).start()

    @pl.loop(0, 16)
    def _(u):
        c = (y + far_first(u >> 1, 8)) & 7
        h = u & 1
        keep = own & (c == y) & (h == core)
        for n, part in enumerate((filt_re, filt_im)):
            source, target = part.at[c, pl.ds(16 * h, 16)], filt_in.at[n, col]

            @pl.when(keep)
            def _():
                pltpu.make_async_copy(source, target, recv_sem.at[4]).start()

            @pl.when(jnp.logical_not(keep))
            def _():
                pltpu.make_async_remote_copy(
                    src_ref=source, dst_ref=target, send_sem=send_sem.at[4], recv_sem=recv_sem.at[4],
                    device_id=(4 * c + zl, 2 * y + h), device_id_type=MESH,
                ).start()

    @pl.loop(0, 32)
    def _(dl):
        sub = lax.broadcasted_iota(jnp.int32, (8, 128), 0)
        k1 = 16 * (dl + 32 * (sub >> 2)) + 4 * (lane >> 5) + (sub & 3)
        n2 = 32 * col_id + (lane & 31)
        angle = (-2.0 * np.pi / SEQ) * (k1 * n2).astype(F32)
        twist[0, dl] = jnp.cos(angle)
        twist[1, dl] = jnp.sin(angle)

    def arrived(buffer, count, n):
        view = buffer.at[pl.ds(0, count)]
        pltpu.make_async_copy(view, view, recv_sem.at[n]).wait()

    for load in loads[1:]:
        load.wait()
    arrived(in1, 31, 0)

    columns = in1[...].astype(F32).reshape(256, 128).astype(BF16)
    for block in range(4):
        part = jnp.dot(first[block], columns, preferred_element_type=F32).reshape(2, 4, 8, 8, 128)
        turned = [[], []]
        for ka in range(4):
            t_re, t_im = turn[0, ka].reshape(8, 8, 128), turn[1, ka].reshape(8, 8, 128)
            turned[0].append(part[0, ka] * t_re - part[1, ka] * t_im)
            turned[1].append(part[0, ka] * t_im + part[1, ka] * t_re)
        summed = []
        for v in turned:
            u = [
                jnp.where(low64, v[e], v[2 + e]) + pltpu.roll(jnp.where(low64, v[2 + e], v[e]), 64, 2)
                for e in range(2)
            ]
            summed.append(
                jnp.where(low32, u[0] + pltpu.roll(u[0], 96, 2), u[1] + pltpu.roll(u[1], 32, 2))
            )
        at = pl.ds(8 * block, 8)
        w_re, w_im = twist[0, at], twist[1, at]
        m_re = summed[0] * w_re - summed[1] * w_im
        m_im = summed[0] * w_im + summed[1] * w_re
        out2[pl.ds(8 * block, 8)] = jnp.where(low4, m_re, pltpu.roll(m_im, 4, 1)).astype(BF16)
        out2[pl.ds(32 + 8 * block, 8)] = jnp.where(low4, pltpu.roll(m_re, 4, 1), m_im).astype(BF16)
    in2[col_id] = out2[freq_id]

    @pl.loop(0, 63)
    def _(u):
        _, d2, device = plane_peer(u)
        pltpu.make_async_remote_copy(
            src_ref=out2.at[d2], dst_ref=in2.at[col_id],
            send_sem=send_sem.at[1], recv_sem=recv_sem.at[1], device_id=device, device_id_type=MESH,
        ).start()

    for n in range(2):
        view = filt_in.at[n]
        if n == 0:
            pltpu.make_async_copy(filt_in, filt_in, recv_sem.at[4]).wait()
        filt_f[n] = filt_in[n].astype(F32).reshape(256, 128)
        for pair in range(2):
            rows = [
                filt_f[n, pl.ds(4 * ka + 2 * pair + e, 16, stride=16), :]
                for e in range(2)
                for ka in range(4)
            ]
            turned = jnp.concatenate(rows, axis=0).T
            upper, lower = turned[:64].reshape(8, 8, 128), turned[64:].reshape(8, 8, 128)
            filt_h[n, 2 * pair] = jnp.where(low64, upper, pltpu.roll(lower, 64, 2)).reshape(64, 128)
            filt_h[n, 2 * pair + 1] = jnp.where(low64, pltpu.roll(upper, 64, 2), lower).reshape(64, 128)

    arrived(in2, 63, 1)

    series = in2[...].astype(F32).reshape(512, 128).astype(BF16)
    part = jnp.dot(wide[...], series, preferred_element_type=F32).reshape(2, 4, 64, 128)
    b_re, b_im = bend[0], bend[1]
    bent = jnp.concatenate(
        [part[0] * b_re - part[1] * b_im, part[0] * b_im + part[1] * b_re], axis=2
    ).reshape(256, 256).astype(BF16)
    spec = jnp.dot(bent, short[...], preferred_element_type=F32)
    s_re, s_im = spec[:, :128], spec[:, 128:]
    h_re, h_im = filt_h[0].reshape(256, 128), filt_h[1].reshape(256, 128)
    prod = jnp.concatenate([s_re * h_re - s_im * h_im, s_re * h_im + s_im * h_re], axis=1).astype(BF16)
    part = jnp.dot(prod, shortb[...], preferred_element_type=F32).reshape(4, 64, 256)
    p_re, p_im = part[:, :, :128], part[:, :, 128:]
    bent = jnp.concatenate(
        [p_re * b_re + p_im * b_im, p_im * b_re - p_re * b_im], axis=0
    ).reshape(512, 128).astype(BF16)
    out3[...] = jnp.dot(wideb[...], bent, preferred_element_type=F32).reshape(64, 8, 128).astype(BF16)
    in3[freq_id] = out3[col_id]

    @pl.loop(0, 63)
    def _(u):
        s2, _, device = plane_peer(u)
        pltpu.make_async_remote_copy(
            src_ref=out3.at[s2], dst_ref=in3.at[freq_id],
            send_sem=send_sem.at[2], recv_sem=recv_sem.at[2], device_id=device, device_id_type=MESH,
        ).start()

    arrived(in3, 63, 2)

    for block in range(4):
        even = in3[pl.ds(8 * block, 8)].astype(F32)
        odd = in3[pl.ds(32 + 8 * block, 8)].astype(F32)
        e_re = jnp.where(low4, even, pltpu.roll(odd, 4, 1))
        e_im = jnp.where(low4, pltpu.roll(even, 4, 1), odd)
        at = pl.ds(8 * block, 8)
        w_re, w_im = twist[0, at], twist[1, at]
        spread = []
        for g in (e_re * w_re + e_im * w_im, e_im * w_re - e_re * w_im):
            u = [jnp.where(low32, g, pltpu.roll(g, 32, 2)), jnp.where(low32, pltpu.roll(g, 96, 2), g)]
            r = [pltpu.roll(a, 64, 2) for a in u]
            spread.append(
                [jnp.where(low64, u[e], r[e]) for e in range(2)]
                + [jnp.where(low64, r[e], u[e]) for e in range(2)]
            )
        for ka in range(4):
            t_re, t_im = turn[0, ka].reshape(8, 8, 128), turn[1, ka].reshape(8, 8, 128)
            g_re, g_im = spread[0][ka], spread[1][ka]
            mixed[block, 0, ka] = (g_re * t_re + g_im * t_im).reshape(64, 128).astype(BF16)
            mixed[block, 1, ka] = (g_im * t_re - g_re * t_im).reshape(64, 128).astype(BF16)
    total = jnp.dot(back[...], mixed[...].reshape(2048, 128), preferred_element_type=F32)
    result = total.reshape(32, 8, 128) * (1.0 / SEQ) + skip[y] * in1[...].astype(F32)
    out4[...] = result.astype(BF16)
    in4[row] = out4[row]

    @pl.loop(0, 31)
    def _(u):
        r2, device = row_peer(u)
        pltpu.make_async_remote_copy(
            src_ref=out4.at[r2], dst_ref=in4.at[row],
            send_sem=send_sem.at[3], recv_sem=recv_sem.at[3], device_id=device, device_id_type=MESH,
        ).start()

    def sent(buffer, count, n):
        view = buffer.at[pl.ds(0, count)]
        pltpu.make_async_copy(view, view, send_sem.at[n]).wait()

    sent(in1, 31, 0)
    sent(out2, 63, 1)
    sent(out3, 63, 2)

    @pl.when(own)
    def _():
        view = filt_in.at[:, pl.ds(0, 15)]
        pltpu.make_async_copy(view, view, send_sem.at[4]).wait()

    @pl.when(jnp.logical_not(own))
    def _():
        pltpu.make_async_copy(filt_in, filt_in, send_sem.at[4]).wait()

    arrived(in4, 31, 3)
    blocks = in4[...].astype(F32).reshape(8, 4, 8, 128)
    out[...] = jnp.concatenate(regroup([blocks[:, b] for b in range(4)]), axis=1).astype(BF16)
    sent(out4, 31, 3)


def solution(mesh):
    consts = tables()
    hbm, vmem = pl.BlockSpec(memory_space=pl.ANY), pl.BlockSpec(memory_space=pltpu.VMEM)
    like = lambda a, kind: pltpu.VMEM(a.shape, kind)
    kinds = (BF16, BF16, F32, BF16, BF16, F32, BF16, BF16)

    def local(signal, filter_real, filter_imag, skip):
        return pl.pallas_call(
            kernel,
            out_shape=jax.ShapeDtypeStruct(signal.shape, BF16),
            in_specs=[hbm] * 3 + [pl.BlockSpec(memory_space=pltpu.SMEM)] + [hbm] * 8,
            out_specs=vmem,
            scratch_shapes=[
                pltpu.VMEM((8, 32, 128), BF16),
                pltpu.VMEM((8, 4, 8, 128), BF16),
                pltpu.VMEM((32, 8, 128), BF16),
                pltpu.VMEM((64, 8, 128), BF16),
                pltpu.VMEM((64, 8, 128), BF16),
                pltpu.VMEM((64, 8, 128), BF16),
                pltpu.VMEM((64, 8, 128), BF16),
                pltpu.VMEM((32, 8, 128), BF16),
                pltpu.VMEM((32, 8, 128), BF16),
                pltpu.VMEM((2, 16, 16, 128), BF16),
                pltpu.VMEM((2, 256, 128), F32),
                pltpu.VMEM((2, 4, 64, 128), F32),
                pltpu.VMEM((2, 32, 8, 128), F32),
                pltpu.VMEM((4, 2, 4, 64, 128), BF16),
                *[like(a, kind) for a, kind in zip(consts, kinds)],
                pltpu.SemaphoreType.DMA((9,)),
                pltpu.SemaphoreType.DMA((5,)),
                pltpu.SemaphoreType.DMA((5,)),
            ],
            compiler_params=pltpu.CompilerParams(
                collective_id=0, has_side_effects=True, vmem_limit_bytes=56 << 20
            ),
        )(signal, filter_real, filter_imag, skip, *consts)

    block = P(None, "row", "col")
    return jax.shard_map(
        local, mesh=mesh, in_specs=(block, block, block, P()), out_specs=block, check_vma=False
    )
```

profile of v0, /device:TPU:1, one launch (start us, length us, event | category | flops | bytes accessed | tf_op | source)
XLA Modules:
  0.0 49.2 jit_solution(6055960006126698709)
XLA Ops:
  0.0 47.7 %shard_map.118 = bf16[8,32,128]{2,1,0:T(8,128)(2,1)} custom-call(bf16[8,32,128]{2,1,0:T(8,128)(2,1)} %signal.1, bf16[8,32,128]{2,1,0:T(8,128)(2,1)} %filt_re.1, bf16[8,32,128]{2,1,0:T(8,128)(2,1)} %filt_im.1, f32[8]{0:T(128)} %skip.1, bf16[4,512,256]{2,1,0:T(8,128)(2,1)} %constant.16.clone.c_first, bf16[256,2048]{1,0:T(8,128)(2,1)} %constant.17.clone.c_back, ...), custom_call_target="tpu_custom_call" | custom-call | tf_op jit(solution)/shard_map/pallas_call | solution.py:323
  47.7 1.5 %copy.14 = bf16[8,32,128]{2,1,0:T(8,128)(2,1)} copy(bf16[8,32,128]{2,1,0:T(8,128)(2,1)} %shard_map.118) | data formatting | bytes 131072
where the time goes:
time: 49.3 us; the launch traced here: 49.2 us
  Pallas kernels  47.7 us (97%)
  local copies, waits for them, and re-layouts  1.47 us (3%)
    pallas_call x1, Pallas kernels, local(): pl.pallas_call(kernel, out_shape=jax.ShapeDtypeStruct(signal.shape, BF16)...  47.7 us
    unnamed x1, local copies, waits for them, and re-layouts  1.47 us

commit v1 on v0

--- a/solution.py
+++ b/solution.py
@@ -43,16 +43,15 @@
         half(first.reshape(2048, 256).T),
         full(turn),
         half(wide),
-        half(wide.T),
+        half(wide.T.reshape(2, 4, 8, 8, 512).transpose(1, 0, 2, 3, 4).reshape(4, 128, 512)),
         full(bend),
         half(short),
         half(short.T),
     )
 
 
-def far_first(step, size):
-    half = (step + 1) >> 1
-    return (size // 2 + jnp.where((step & 1) == 1, -half, half)) & (size - 1)
+FAR8 = (4, 3, 5, 2, 6, 1, 7, 0)
+FAR4 = (2, 1, 3, 0)
 
 
 def kernel(
@@ -79,34 +78,39 @@
     for load in loads:
         load.start()
 
-    def row_peer(u):
-        r2 = (((y + far_first(u >> 2, 8)) & 7) << 2) | ((zl + 3 - (u & 3)) & 3)
-        return r2, (r2, col)
-
-    def plane_peer(u):
-        z2 = (z + far_first(u >> 3, 8)) & 7
-        x2 = (xs + far_first((u >> 1) & 3, 4)) & 3
-        zl2, col2 = z2 & 3, ((z2 >> 2) << 3) | (x2 << 1) | (core ^ 1 ^ (u & 1))
-        return 4 * col2 + zl2, 8 * (col2 >> 1) + 2 * zl2 + (col2 & 1), (4 * y + zl2, col2)
+    row_peers = []
+    for dy in FAR8:
+        for dz in (3, 2, 1, 0):
+            y2, zl2 = (y + dy) & 7, (zl + dz) & 3
+            row_peers.append((y2, zl2, (4 * y2 + zl2, col)))
+    planes = []
+    for dx in FAR4:
+        planes.append([])
+        for dz in FAR8:
+            for dc in (1, 0):
+                z2, x2, core2 = (z + dz) & 7, (xs + dx) & 3, core ^ dc
+                zl2, col2 = z2 & 3, ((z2 >> 2) << 3) | (x2 << 1) | core2
+                planes[-1].append((x2, z2, core2, (4 * y + zl2, col2)))
+    cols = []
+    for dz in (1, 0):
+        for dx in FAR4:
+            for dc in (1, 0):
+                cols.append((col ^ (8 * dz + dc)) & 9 | (((xs + dx) & 3) << 1))
 
     own = (col >> 1) == y
     barrier = pltpu.get_barrier_semaphore()
-
-    @pl.loop(0, 31)
-    def _(u):
-        pl.semaphore_signal(barrier, inc=1, device_id=row_peer(u)[1], device_id_type=MESH)
-
-    @pl.loop(0, 63)
-    def _(u):
-        pl.semaphore_signal(barrier, inc=1, device_id=plane_peer(u)[2], device_id_type=MESH)
-
-    @pl.loop(0, 16)
-    def _(u):
-        @pl.when(jnp.logical_not(own & (u == col)))
-        def _():
-            pl.semaphore_signal(
-                barrier, inc=1, device_id=(4 * (col >> 1) + zl, u), device_id_type=MESH
-            )
+    hear = lambda device: pl.semaphore_signal(barrier, inc=1, device_id=device, device_id_type=MESH)
+    for col2 in cols[:-1]:
+        hear((4 * (col >> 1) + zl, col2))
+
+    @pl.when(jnp.logical_not(own))
+    def _():
+        hear((4 * (col >> 1) + zl, col))
+
+    for peer in row_peers[:-1]:
+        hear(peer[-1])
+    for peer in sum(planes, [])[:-1]:
+        hear(peer[-1])
 
     lane = lax.broadcasted_iota(jnp.int32, (8, 128), 1)
     low64, low32 = lane < 64, (lane & 32) == 0
@@ -131,35 +135,31 @@
 
     pl.semaphore_wait(barrier, 31 + 63 + 16 - own.astype(jnp.int32))
 
-    def send1(u):
-        r2, device = row_peer(u)
-        return pltpu.make_async_remote_copy(
-            src_ref=out1.at[r2 >> 2, r2 & 3], dst_ref=in1.at[row],
-            send_sem=send_sem.at[0], recv_sem=recv_sem.at[0], device_id=device, device_id_type=MESH,
-        )
-
-    @pl.loop(0, 31)
-    def _(u):
-        send1(u).start()
-
-    @pl.loop(0, 16)
-    def _(u):
-        c = (y + far_first(u >> 1, 8)) & 7
-        h = u & 1
-        keep = own & (c == y) & (h == core)
-        for n, part in enumerate((filt_re, filt_im)):
-            source, target = part.at[c, pl.ds(16 * h, 16)], filt_in.at[n, col]
-
-            @pl.when(keep)
-            def _():
-                pltpu.make_async_copy(source, target, recv_sem.at[4]).start()
-
-            @pl.when(jnp.logical_not(keep))
-            def _():
-                pltpu.make_async_remote_copy(
-                    src_ref=source, dst_ref=target, send_sem=send_sem.at[4], recv_sem=recv_sem.at[4],
-                    device_id=(4 * c + zl, 2 * y + h), device_id_type=MESH,
-                ).start()
+    def send(source, target, n, device):
+        pltpu.make_async_remote_copy(
+            src_ref=source, dst_ref=target, send_sem=send_sem.at[n], recv_sem=recv_sem.at[n],
+            device_id=device, device_id_type=MESH,
+        ).start()
+
+    for y2, zl2, device in row_peers[:-1]:
+        send(out1.at[y2, zl2], in1.at[row], 0, device)
+
+    for dy in FAR8:
+        for dc in (1, 0):
+            c, h = (y + dy) & 7, core ^ dc
+            for n, part in enumerate((filt_re, filt_im)):
+                source, target = part.at[c, pl.ds(16 * h, 16)], filt_in.at[n, col]
+                if dy or dc:
+                    send(source, target, 4, (4 * c + zl, 2 * y + h))
+                    continue
+
+                @pl.when(own)
+                def _():
+                    pltpu.make_async_copy(source, target, recv_sem.at[4]).start()
+
+                @pl.when(jnp.logical_not(own))
+                def _():
+                    send(source, target, 4, (4 * c + zl, 2 * y + h))
 
     @pl.loop(0, 32)
     def _(dl):
@@ -179,7 +179,8 @@
     arrived(in1, 31, 0)
 
     columns = in1[...].astype(F32).reshape(256, 128).astype(BF16)
-    for block in range(4):
+    for peers in planes:
+        block = peers[0][0]
         part = jnp.dot(first[block], columns, preferred_element_type=F32).reshape(2, 4, 8, 8, 128)
         turned = [[], []]
         for ka in range(4):
@@ -201,15 +202,12 @@
         m_im = summed[0] * w_im + summed[1] * w_re
         out2[pl.ds(8 * block, 8)] = jnp.where(low4, m_re, pltpu.roll(m_im, 4, 1)).astype(BF16)
         out2[pl.ds(32 + 8 * block, 8)] = jnp.where(low4, pltpu.roll(m_re, 4, 1), m_im).astype(BF16)
-    in2[col_id] = out2[freq_id]
-
-    @pl.loop(0, 63)
-    def _(u):
-        _, d2, device = plane_peer(u)
-        pltpu.make_async_remote_copy(
-            src_ref=out2.at[d2], dst_ref=in2.at[col_id],
-            send_sem=send_sem.at[1], recv_sem=recv_sem.at[1], device_id=device, device_id_type=MESH,
-        ).start()
+        for x2, z2, core2, device in peers:
+            d2 = ((z2 >> 2) << 5) | (x2 << 3) | ((z2 & 3) << 1) | core2
+            if peers is planes[-1] and device is peers[-1][-1]:
+                in2[col_id] = out2[d2]
+            else:
+                send(out2.at[d2], in2.at[col_id], 1, device)
 
     for n in range(2):
         view = filt_in.at[n]
@@ -244,16 +242,16 @@
     bent = jnp.concatenate(
         [p_re * b_re + p_im * b_im, p_im * b_re - p_re * b_im], axis=0
     ).reshape(512, 128).astype(BF16)
-    out3[...] = jnp.dot(wideb[...], bent, preferred_element_type=F32).reshape(64, 8, 128).astype(BF16)
-    in3[freq_id] = out3[col_id]
-
-    @pl.loop(0, 63)
-    def _(u):
-        s2, _, device = plane_peer(u)
-        pltpu.make_async_remote_copy(
-            src_ref=out3.at[s2], dst_ref=in3.at[freq_id],
-            send_sem=send_sem.at[2], recv_sem=recv_sem.at[2], device_id=device, device_id_type=MESH,
-        ).start()
+    for peers in planes:
+        block = peers[0][0]
+        part = jnp.dot(wideb[block], bent, preferred_element_type=F32)
+        out3[block] = part.reshape(16, 8, 128).astype(BF16)
+        for x2, z2, core2, device in peers:
+            s2 = ((z2 >> 2) << 3) | (core2 << 2) | (z2 & 3)
+            if peers is planes[-1] and device is peers[-1][-1]:
+                in3[freq_id] = out3[block, s2]
+            else:
+                send(out3.at[block, s2], in3.at[freq_id], 2, device)
 
     arrived(in3, 63, 2)
 
@@ -282,13 +280,8 @@
     out4[...] = result.astype(BF16)
     in4[row] = out4[row]
 
-    @pl.loop(0, 31)
-    def _(u):
-        r2, device = row_peer(u)
-        pltpu.make_async_remote_copy(
-            src_ref=out4.at[r2], dst_ref=in4.at[row],
-            send_sem=send_sem.at[3], recv_sem=recv_sem.at[3], device_id=device, device_id_type=MESH,
-        ).start()
+    for y2, zl2, device in row_peers[:-1]:
+        send(out4.at[4 * y2 + zl2], in4.at[row], 3, device)
 
     def sent(buffer, count, n):
         view = buffer.at[pl.ds(0, count)]
@@ -296,7 +289,7 @@
 
     sent(in1, 31, 0)
     sent(out2, 63, 1)
-    sent(out3, 63, 2)
+    sent(in3, 63, 2)
 
     @pl.when(own)
     def _():
@@ -331,7 +324,7 @@
                 pltpu.VMEM((32, 8, 128), BF16),
                 pltpu.VMEM((64, 8, 128), BF16),
                 pltpu.VMEM((64, 8, 128), BF16),
-                pltpu.VMEM((64, 8, 128), BF16),
+                pltpu.VMEM((4, 16, 8, 128), BF16),
                 pltpu.VMEM((64, 8, 128), BF16),
                 pltpu.VMEM((32, 8, 128), BF16),
                 pltpu.VMEM((32, 8, 128), BF16),

time: 49.3 us -> 46.9 us (0.951)
  Pallas kernels: 47.7 us -> 45.3 us
    pallas_call x1, Pallas kernels: 47.7 us -> 45.3 us  [local(): pl.pallas_call(kernel, out_shape=jax.ShapeDtypeStruct(signal.shape, BF16)...]
where the time goes in v1:
time: 46.9 us; the launch traced here: 46.8 us
  Pallas kernels  45.3 us (97%)
  local copies, waits for them, and re-layouts  1.47 us (3%)
    pallas_call x1, Pallas kernels, local(): pl.pallas_call(kernel, out_shape=jax.ShapeDtypeStruct(signal.shape, BF16)...  45.3 us
    unnamed x1, local copies, waits for them, and re-layouts  1.47 us

profile of v1, /device:TPU:1, one launch (start us, length us, event | category | flops | bytes accessed | tf_op | source)
XLA Modules:
  0.0 46.8 jit_solution(10490758534732617825)
XLA Ops:
  0.0 45.3 %shard_map.118 = bf16[8,32,128]{2,1,0:T(8,128)(2,1)} custom-call(bf16[8,32,128]{2,1,0:T(8,128)(2,1)} %signal.1, bf16[8,32,128]{2,1,0:T(8,128)(2,1)} %filt_re.1, bf16[8,32,128]{2,1,0:T(8,128)(2,1)} %filt_im.1, f32[8]{0:T(128)} %skip.1, bf16[4,512,256]{2,1,0:T(8,128)(2,1)} %constant.16.clone.c_first, bf16[256,2048]{1,0:T(8,128)(2,1)} %constant.17.clone.c_back, ...), custom_call_target="tpu_custom_call" | custom-call | tf_op jit(solution)/shard_map/pallas_call | solution.py:316
  45.3 1.5 %copy.14 = bf16[8,32,128]{2,1,0:T(8,128)(2,1)} copy(bf16[8,32,128]{2,1,0:T(8,128)(2,1)} %shard_map.118) | data formatting | bytes 131072

commit v2 on v1

--- a/solution.py
+++ b/solution.py
@@ -12,6 +12,7 @@
 F32, BF16 = jnp.float32, jnp.bfloat16
 N1, N2 = 1024, 2048
 SEQ = N1 * N2
+VMEM_BYTES = 55142 << 10
 
 
 def unit(product, modulus):
@@ -55,7 +56,7 @@
 
 
 def kernel(
-    signal, filt_re, filt_im, skip,
+    signal, filt_re, filt_im,
     c_first, c_back, c_turn, c_wide, c_wideb, c_bend, c_short, c_shortb,
     out,
     x_in, out1, in1, out2, in2, out3, in3, out4, in4, filt_in, filt_f, filt_h, twist, mixed,
@@ -75,8 +76,7 @@
             (c_short, short), (c_shortb, shortb), (c_wideb, wideb), (c_back, back),
         ))
     ]
-    for load in loads:
-        load.start()
+    loads[0].start()
 
     row_peers = []
     for dy in FAR8:
@@ -126,6 +126,9 @@
             v.append(jnp.where(low32, u[b][0], pltpu.roll(u[b][1], 32, 2)))
             v.append(jnp.where(low32, pltpu.roll(u[b][0], 96, 2), u[b][1]))
         return v
+
+    for load in loads[1:]:
+        load.start()
 
     loads[0].wait()
     pieces = x_in[...].astype(F32)
@@ -276,7 +279,7 @@
             mixed[block, 0, ka] = (g_re * t_re + g_im * t_im).reshape(64, 128).astype(BF16)
             mixed[block, 1, ka] = (g_im * t_re - g_re * t_im).reshape(64, 128).astype(BF16)
     total = jnp.dot(back[...], mixed[...].reshape(2048, 128), preferred_element_type=F32)
-    result = total.reshape(32, 8, 128) * (1.0 / SEQ) + skip[y] * in1[...].astype(F32)
+    result = total.reshape(32, 8, 128) * (1.0 / SEQ)
     out4[...] = result.astype(BF16)
     in4[row] = out4[row]
 
@@ -313,10 +316,10 @@
     kinds = (BF16, BF16, F32, BF16, BF16, F32, BF16, BF16)
 
     def local(signal, filter_real, filter_imag, skip):
-        return pl.pallas_call(
+        conv = pl.pallas_call(
             kernel,
             out_shape=jax.ShapeDtypeStruct(signal.shape, BF16),
-            in_specs=[hbm] * 3 + [pl.BlockSpec(memory_space=pltpu.SMEM)] + [hbm] * 8,
+            in_specs=[hbm] * 11,
             out_specs=vmem,
             scratch_shapes=[
                 pltpu.VMEM((8, 32, 128), BF16),
@@ -339,9 +342,10 @@
                 pltpu.SemaphoreType.DMA((5,)),
             ],
             compiler_params=pltpu.CompilerParams(
-                collective_id=0, has_side_effects=True, vmem_limit_bytes=56 << 20
+                collective_id=0, has_side_effects=True, vmem_limit_bytes=VMEM_BYTES
             ),
-        )(signal, filter_real, filter_imag, skip, *consts)
+        )(signal, filter_real, filter_imag, *consts)
+        return (conv.astype(F32) + skip[:, None, None] * signal.astype(F32)).astype(BF16)
 
     block = P(None, "row", "col")
     return jax.shard_map(

time: 46.9 us -> 45 us (0.959)
  local copies, waits for them, and re-layouts: 1.47 us -> 0.01 us
  Pallas kernels: 45.3 us -> 44.1 us
  other arithmetic: 0 us -> 0.72 us
    unnamed x1 -> x4, local copies, waits for them, and re-layouts: 1.47 us -> 0.01 us
    pallas_call x1, Pallas kernels: 45.3 us -> 44.1 us  [local(): pl.pallas_call(kernel, out_shape=jax.ShapeDtypeStruct(signal.shape, BF16)...]
    convert_element_type x0 -> x1, other arithmetic: none -> 0.72 us  [local(): (conv.astype(F32) + skip[:, None, None] * signal.astype(F32)).astype(BF16)]
where the time goes in v2:
time: 45 us; the launch traced here: 44.9 us
  Pallas kernels  44.1 us (98%)
  other arithmetic  0.72 us (2%)
    pallas_call x1, Pallas kernels, local(): pl.pallas_call(kernel, out_shape=jax.ShapeDtypeStruct(signal.shape, BF16)...  44.1 us

profile of v2, /device:TPU:1, one launch (start us, length us, event | category | flops | bytes accessed | tf_op | source)
XLA Modules:
  0.0 44.9 jit_solution(2175951309571884475)
XLA Ops:
  0.0 0.0 copy-start
  0.0 0.0 copy-start.1
  0.0 44.1 %shard_map.118 = bf16[8,32,128]{2,1,0:T(8,128)(2,1)S(1)} custom-call(bf16[8,32,128]{2,1,0:T(8,128)(2,1)} %signal.1, bf16[8,32,128]{2,1,0:T(8,128)(2,1)} %filt_re.1, bf16[8,32,128]{2,1,0:T(8,128)(2,1)} %filt_im.1, bf16[4,512,256]{2,1,0:T(8,128)(2,1)} %constant.16.clone.c_first, bf16[256,2048]{1,0:T(8,128)(2,1)} %constant.17.clone.c_back, ...), custom_call_target="tpu_custom_call" | custom-call | tf_op jit(solution)/shard_map/pallas_call | solution.py:319
  44.2 0.0 copy-done
  44.2 0.0 copy-done.1
  44.2 0.7 %add_convert_fusion = bf16[8,32,128]{2,1,0:T(8,128)(2,1)} fusion(bf16[8,32,128]{2,1,0:T(8,128)(2,1)S(1)} %copy-done, bf16[8,32,128]{2,1,0:T(8,128)(2,1)S(1)} %shard_map.118, f32[8]{0:T(128)S(1)} %copy-done.1), kind=kLoop, calls=%fused_computation | loop fusion | flops 163840 | bytes 196640 | tf_op jit(solution)/shard_map/convert_element_type | solution.py:348
Async XLA Ops:
  0.0 44.2 %copy-start = (bf16[8,32,128]{2,1,0:T(8,128)(2,1)S(1)}, bf16[8,32,128]{2,1,0:T(8,128)(2,1)}, u32[]{:S(2)}) copy-start(bf16[8,32,128]{2,1,0:T(8,128)(2,1)} %signal.1) | copy-start | bytes 196612
  0.0 44.2 %copy-start.1 = (f32[8]{0:T(128)S(1)}, f32[8]{0:T(128)}, u32[]{:S(2)}) copy-start(f32[8]{0:T(128)} %param.15) | copy-start | bytes 100

commit v3 on v2

--- a/solution.py
+++ b/solution.py
@@ -67,7 +67,8 @@
     y, zl = row >> 2, row & 3
     z, xs, core = ((col >> 3) << 2) | zl, (col >> 1) & 3, col & 1
     col_id = 4 * col + zl
-    freq_id = 8 * (col >> 1) + 2 * zl + core
+    half = zl ^ 2
+    freq_id = 8 * (col >> 1) + 2 * half + core
 
     loads = [
         pltpu.make_async_copy(a, b, load_sem.at[n])
@@ -97,16 +98,10 @@
             for dc in (1, 0):
                 cols.append((col ^ (8 * dz + dc)) & 9 | (((xs + dx) & 3) << 1))
 
-    own = (col >> 1) == y
     barrier = pltpu.get_barrier_semaphore()
     hear = lambda device: pl.semaphore_signal(barrier, inc=1, device_id=device, device_id_type=MESH)
-    for col2 in cols[:-1]:
-        hear((4 * (col >> 1) + zl, col2))
-
-    @pl.when(jnp.logical_not(own))
-    def _():
-        hear((4 * (col >> 1) + zl, col))
-
+    for col2 in cols:
+        hear((4 * (col >> 1) + half, col2))
     for peer in row_peers[:-1]:
         hear(peer[-1])
     for peer in sum(planes, [])[:-1]:
@@ -136,7 +131,7 @@
         out1[:, b] = piece.astype(BF16)
     in1[row] = out1[y, zl]
 
-    pl.semaphore_wait(barrier, 31 + 63 + 16 - own.astype(jnp.int32))
+    pl.semaphore_wait(barrier, 31 + 63 + 16)
 
     def send(source, target, n, device):
         pltpu.make_async_remote_copy(
@@ -152,17 +147,7 @@
             c, h = (y + dy) & 7, core ^ dc
             for n, part in enumerate((filt_re, filt_im)):
                 source, target = part.at[c, pl.ds(16 * h, 16)], filt_in.at[n, col]
-                if dy or dc:
-                    send(source, target, 4, (4 * c + zl, 2 * y + h))
-                    continue
-
-                @pl.when(own)
-                def _():
-                    pltpu.make_async_copy(source, target, recv_sem.at[4]).start()
-
-                @pl.when(jnp.logical_not(own))
-                def _():
-                    send(source, target, 4, (4 * c + zl, 2 * y + h))
+                send(source, target, 4, (4 * c + half, 2 * y + h))
 
     @pl.loop(0, 32)
     def _(dl):
@@ -206,7 +191,7 @@
         out2[pl.ds(8 * block, 8)] = jnp.where(low4, m_re, pltpu.roll(m_im, 4, 1)).astype(BF16)
         out2[pl.ds(32 + 8 * block, 8)] = jnp.where(low4, pltpu.roll(m_re, 4, 1), m_im).astype(BF16)
         for x2, z2, core2, device in peers:
-            d2 = ((z2 >> 2) << 5) | (x2 << 3) | ((z2 & 3) << 1) | core2
+            d2 = ((z2 >> 2) << 5) | (x2 << 3) | (((z2 & 3) ^ 2) << 1) | core2
             if peers is planes[-1] and device is peers[-1][-1]:
                 in2[col_id] = out2[d2]
             else:
@@ -294,15 +279,7 @@
     sent(out2, 63, 1)
     sent(in3, 63, 2)
 
-    @pl.when(own)
-    def _():
-        view = filt_in.at[:, pl.ds(0, 15)]
-        pltpu.make_async_copy(view, view, send_sem.at[4]).wait()
-
-    @pl.when(jnp.logical_not(own))
-    def _():
-        pltpu.make_async_copy(filt_in, filt_in, send_sem.at[4]).wait()
-
+    pltpu.make_async_copy(filt_in, filt_in, send_sem.at[4]).wait()
     arrived(in4, 31, 3)
     blocks = in4[...].astype(F32).reshape(8, 4, 8, 128)
     out[...] = jnp.concatenate(regroup([blocks[:, b] for b in range(4)]), axis=1).astype(BF16)

time: 45 us -> 44.2 us (0.982)
  Pallas kernels: 44.1 us -> 43.4 us
    pallas_call x1, Pallas kernels: 44.1 us -> 43.4 us  [local(): pl.pallas_call(kernel, out_shape=jax.ShapeDtypeStruct(signal.shape, BF16)...]
where the time goes in v3:
time: 44.2 us; the launch traced here: 44.1 us
  Pallas kernels  43.4 us (98%)
  other arithmetic  0.72 us (2%)
    pallas_call x1, Pallas kernels, local(): pl.pallas_call(kernel, out_shape=jax.ShapeDtypeStruct(signal.shape, BF16)...  43.4 us

profile of v3, /device:TPU:1, one launch (start us, length us, event | category | flops | bytes accessed | tf_op | source)
XLA Modules:
  0.0 44.1 jit_solution(16678537617446404408)
XLA Ops:
  0.0 0.0 copy-start
  0.0 0.0 copy-start.1
  0.0 43.4 %shard_map.118 = bf16[8,32,128]{2,1,0:T(8,128)(2,1)S(1)} custom-call(bf16[8,32,128]{2,1,0:T(8,128)(2,1)} %signal.1, bf16[8,32,128]{2,1,0:T(8,128)(2,1)} %filt_re.1, bf16[8,32,128]{2,1,0:T(8,128)(2,1)} %filt_im.1, bf16[4,512,256]{2,1,0:T(8,128)(2,1)} %constant.16.clone.c_first, bf16[256,2048]{1,0:T(8,128)(2,1)} %constant.17.clone.c_back, ...), custom_call_target="tpu_custom_call" | custom-call | tf_op jit(solution)/shard_map/pallas_call | solution.py:296
  43.4 0.0 copy-done
  43.4 0.0 copy-done.1
  43.4 0.7 %add_convert_fusion = bf16[8,32,128]{2,1,0:T(8,128)(2,1)} fusion(bf16[8,32,128]{2,1,0:T(8,128)(2,1)S(1)} %copy-done, bf16[8,32,128]{2,1,0:T(8,128)(2,1)S(1)} %shard_map.118, f32[8]{0:T(128)S(1)} %copy-done.1), kind=kLoop, calls=%fused_computation | loop fusion | flops 163840 | bytes 196640 | tf_op jit(solution)/shard_map/convert_element_type | solution.py:325
Async XLA Ops:
  0.0 43.4 %copy-start = (bf16[8,32,128]{2,1,0:T(8,128)(2,1)S(1)}, bf16[8,32,128]{2,1,0:T(8,128)(2,1)}, u32[]{:S(2)}) copy-start(bf16[8,32,128]{2,1,0:T(8,128)(2,1)} %signal.1) | copy-start | bytes 196612
  0.0 43.4 %copy-start.1 = (f32[8]{0:T(128)S(1)}, f32[8]{0:T(128)}, u32[]{:S(2)}) copy-start(f32[8]{0:T(128)} %param.15) | copy-start | bytes 100
